TPU v7x, 32 devices: a whole 2x2x4 slice. The times are simulated.
32 devices in a mesh: sec: 4 (over y, x), dom: 8 (over z, core).
Axes of the slice: x: 2, y: 2, z: 4, core: 2. Of those that a mesh axis runs over, the one named last changes fastest.
Arguments:
- fields: float32 [4, 64, 8192], P(None, None, ('sec', 'dom')), may hold values from -6 to 6
- source_map: int32 [8192], P(('sec', 'dom')), may hold values from 0 to 255
- new_owner: int32 [2048], P(('sec', 'dom')), may hold values from 0 to 7, as said below
- send_list: int32 [3072], P(('sec', 'dom')), may hold values from -1 to 1535, as said below
- face_slot: int32 [6, 8192], P(None, ('sec', 'dom')), may hold values from -1 to 1631, as said below
Outputs:
- advanced: float32 [4, 64, 8192], P(None, None, ('sec', 'dom'))
Inputs may be any that keep to these rules, and one draw needn't show every extreme that they name: source_map names a cell block of the flow device with the same dom index. new_owner names a device of the same section within 2 dom indices; two devices trade as many blocks each way, at most 4; in every section some device trades exactly 4 with each of its 4 nearby devices. send_list holds, for each device, 4 lists of 24 entries for the offsets -2 to -1 and 1 to 2; an entry f * 256 + e names face f of local element e; a list for a device inside the section is full, one for a device outside it is -1. face_slot names for every element face the touching face: the opposite end along the same direction, nodes in the same order, on the same device or in the lists of a device within 2; -1 marks the outer boundary.
All inputs are finite; a program needn't handle non-finite values.
Results may differ from a plain program's by a relative error of at most 0.0003.
Values sent between devices are 32-bit elements; how exact they have to be, the bound alone decides.
A program may use at most 64 MiB of HBM per device.

v0:
```python
import functools

import jax
import jax.numpy as jnp
import numpy as np
from jax import lax
from jax.experimental import pallas as pl
from jax.experimental.pallas import tpu as pltpu
from jax.sharding import PartitionSpec as P

BLOCK_SIZE = 4
MOVE_CAP = 4
SPREAD = 2
FACE_CAP = 24
MOVE = MOVE_CAP * BLOCK_SIZE
PEERS = 2 * SPREAD
LANES = 128
TRACE = 48
OFFSETS = [value for value in range(-SPREAD, SPREAD + 1) if value != 0]

CELL_DIFFERENCE = [
    [-1.0, 1.0, 0.0, 0.0],
    [-0.5, 0.0, 0.5, 0.0],
    [0.0, -0.5, 0.0, 0.5],
    [0.0, 0.0, -1.0, 1.0],
]
SEGMENT_CARRY = [
    0.0,
    -567301805773.0 / 1357537059087.0,
    -2404267990393.0 / 2016746695238.0,
    -3550918686646.0 / 2091501179385.0,
    -1275806237668.0 / 842570457699.0,
]
SEGMENT_WEIGHTS = [
    1432997174477.0 / 9575080441755.0,
    5161836677717.0 / 13612068292357.0,
    1720146321549.0 / 2090206949498.0,
    3134564353537.0 / 4481467310338.0,
    2277821191437.0 / 14882151754819.0,
]
SEGMENTS = len(SEGMENT_CARRY)
TIME_STEP = 0.12
END_LIFT = 6.0
F32 = jnp.float32
BF16 = jnp.bfloat16
MESH = pl.DeviceIdType.MESH


def node_derivative():
    points = np.array([-1.0, -1.0 / np.sqrt(5.0), 1.0 / np.sqrt(5.0), 1.0])
    products = np.array(
        [np.prod([points[row] - points[col] for col in range(4) if col != row]) for row in range(4)]
    )
    matrix = np.zeros((4, 4))
    for row in range(4):
        for col in range(4):
            if row != col:
                matrix[row, col] = products[row] / (products[col] * (points[row] - points[col]))
        matrix[row, row] = -np.sum(matrix[row])
    return matrix


def along(matrix, direction):
    parts = [np.eye(4)] * 3
    parts[direction] = matrix
    return np.kron(np.kron(parts[0], parts[1]), parts[2])


def face_nodes(direction, side):
    cube = np.arange(64).reshape(4, 4, 4)
    return np.take(cube, 3 * side, axis=direction).reshape(-1)


def constants():
    deriv = node_derivative()
    own = np.zeros((256, 256))
    lift = np.zeros((256, 6 * TRACE))
    pick = np.zeros((6 * TRACE, 256))
    half = 0.5 * END_LIFT
    for a in range(3):
        va = 64 * (1 + a)
        own[:64, va : va + 64] -= along(deriv, a)
        own[va : va + 64, :64] -= along(deriv, a)
        others = [64 * (1 + b) for b in range(3) if b != a]
        for side in range(2):
            face = 2 * a + side
            sign = 2.0 * side - 1.0
            for number, n in enumerate(face_nodes(a, side)):
                own[n, n] -= half
                own[n, va + n] += half * sign
                own[va + n, va + n] -= half
                own[va + n, n] += half * sign
                at = TRACE * face + number
                lift[n, at] = half
                lift[va + n, at] = -half * sign
                pick[at, n] = 1.0
                pick[at, va + n] = sign
                for place, row in enumerate(others):
                    own[row + n, row + n] -= half
                    lift[row + n, at + 16 * (1 + place)] = half
                    pick[at + 16 * (1 + place), row + n] = 1.0
    diff = np.array(CELL_DIFFERENCE)
    curl = np.zeros((192, 192))
    for a in range(3):
        b, c = (a + 1) % 3, (a + 2) % 3
        curl[64 * a : 64 * a + 64, 64 * c : 64 * c + 64] += along(diff, b)
        curl[64 * a : 64 * a + 64, 64 * b : 64 * b + 64] -= along(diff, c)
    own = own.astype(np.float32)
    own_high = own.astype(jnp.bfloat16)
    own_low = (own - own_high.astype(np.float32)).astype(jnp.bfloat16)
    return [m.astype(jnp.bfloat16) for m in (own_high, own_low, lift, pick, curl)]


def slot_number(offset):
    return offset + SPREAD if offset < 0 else offset + SPREAD - 1


def split(value):
    high = value.astype(BF16)
    return high, (value - high.astype(F32)).astype(BF16)


def dot(a, b):
    return jnp.dot(a, b, preferred_element_type=F32)


def dot_nt(a, b):
    return lax.dot_general(a, b, (((1,), (1,)), ((), ())), preferred_element_type=F32)


def ones_where(condition):
    return jnp.where(condition, 1.0, 0.0).astype(BF16)


def rows_of(shape):
    return lax.broadcasted_iota(jnp.int32, shape, 0)


def lanes_of(shape):
    return lax.broadcasted_iota(jnp.int32, shape, 1)


def kernel(
    n_sec, n_dom,
    fields, source_map, new_owner, send_list, face_slot,
    own_high, own_low, lift, pick, curl,
    out,
    carry, force, lamb, near, far, sends, row_list,
    move_out, move_in, force_out, force_in, sent, received,
    lamb_send, lamb_recv, move_send, move_recv, force_send, force_recv, face_send, face_recv,
):
    sec, me = lax.axis_index("sec"), lax.axis_index("dom")
    elements = fields.shape[1]
    blocks = new_owner.shape[1]
    flow = sec == 0
    acoustic = sec > 0
    inside = [(me + o >= 0) & (me + o < n_dom) for o in OFFSETS]

    barrier = pltpu.get_barrier_semaphore()
    greeted = jnp.where(flow, n_sec - 1, 1)
    for slot, o in enumerate(OFFSETS):
        greeted = greeted + jnp.where(inside[slot], 1, 0)

        @pl.when(inside[slot])
        def _():
            pl.semaphore_signal(barrier, inc=1, device_id=(sec, me + o), device_id_type=MESH)

    @pl.when(flow)
    def _():
        for other in range(1, n_sec):
            pl.semaphore_signal(barrier, inc=1, device_id=(other, me), device_id_type=MESH)

    @pl.when(acoustic)
    def _():
        pl.semaphore_signal(barrier, inc=1, device_id=(0, me), device_id_type=MESH)

    def lamb_copy(chunk, other):
        part = lamb.at[pl.ds(64 * chunk, 64)]
        return pltpu.make_async_remote_copy(
            src_ref=part,
            dst_ref=part,
            send_sem=lamb_send.at[chunk, other - 1],
            recv_sem=lamb_recv.at[chunk],
            device_id=(other, me),
            device_id_type=MESH,
        )

    def peer_copy(source, target, send_sem, recv_sem, slot):
        there = PEERS - 1 - slot
        return pltpu.make_async_remote_copy(
            src_ref=source,
            dst_ref=target.at[there],
            send_sem=send_sem.at[slot],
            recv_sem=recv_sem.at[there],
            device_id=(sec, me + OFFSETS[slot]),
            device_id_type=MESH,
        )

    def start_all(copies):
        for slot in range(PEERS):

            @pl.when(inside[slot])
            def _():
                copies(slot).start()

    def wait_recv_all(target, recv_sem, send_sem):
        for slot in range(PEERS):

            @pl.when(inside[slot])
            def _():
                pltpu.make_async_remote_copy(
                    src_ref=target.at[slot],
                    dst_ref=target.at[slot],
                    send_sem=send_sem.at[slot],
                    recv_sem=recv_sem.at[slot],
                    device_id=(sec, me + OFFSETS[slot]),
                    device_id_type=MESH,
                ).wait_recv()

    def wait_send_all(copies):
        for slot in range(PEERS):

            @pl.when(inside[slot])
            def _():
                copies(slot).wait_send()

    @pl.when(flow)
    def _():
        high, low = split(fields[0:192, :])
        spin = dot(curl[...], high) + dot(curl[...], low)
        u = [fields[64 * a : 64 * a + 64, :] for a in range(3)]
        w = [spin[64 * a : 64 * a + 64, :] for a in range(3)]
        rho = fields[192:256, :]
        for a in range(3):
            b, c = (a + 1) % 3, (a + 2) % 3
            lamb[64 * a : 64 * a + 64, :] = rho * (w[b] * u[c] - w[c] * u[b])

    spread_shape = (blocks, elements)
    spread = ones_where(lanes_of(spread_shape) // BLOCK_SIZE == rows_of(spread_shape))
    owner = jnp.broadcast_to((new_owner[...] - me).astype(F32), (8, blocks)).astype(BF16)
    away = dot(owner, spread)
    group = rows_of((8, elements))
    wanted = jnp.where(group <= SPREAD, group - SPREAD - 1, group - SPREAD)
    wanted = jnp.where(group == 0, 0, jnp.where(group > PEERS, 99, wanted)).astype(F32)
    match = jnp.where(away == wanted, 1.0, 0.0)
    square = (elements, elements)
    before = ones_where(rows_of(square) < lanes_of(square))
    place = dot(match.astype(BF16), before)
    counts = jnp.sum(match, axis=1, keepdims=True)
    keep_match = jnp.where(group == 0, match, 0.0)
    move_match = match - keep_match
    base = (MOVE * (group - 1)).astype(F32)
    kept = jnp.sum(keep_match * (place + 1.0), axis=0, keepdims=True).astype(jnp.int32) - 1
    moved = jnp.sum(move_match * (place + base + 1.0), axis=0, keepdims=True).astype(jnp.int32) - 1
    total = PEERS * MOVE
    move_sel = ones_where(rows_of((total, elements)) == moved)

    field_high, field_low = split(fields[...])
    outgoing = dot_nt(move_sel, field_high) + dot_nt(move_sel, field_low)
    for slot in range(PEERS):
        move_out[slot] = outgoing[MOVE * slot : MOVE * slot + MOVE, :]

    def moves(slot):
        return peer_copy(move_out.at[slot], move_in, move_send, move_recv, slot)

    pl.semaphore_wait(barrier, greeted)
    start_all(moves)

    @pl.when(flow)
    def _():
        for chunk in range(3):
            for other in range(1, n_sec):
                lamb_copy(chunk, other).start()

    for slot in range(PEERS):

        @pl.when(jnp.logical_not(inside[slot]))
        def _():
            move_in[slot] = jnp.zeros(move_in.shape[1:], F32)
            force_in[slot] = jnp.zeros(force_in.shape[1:], F32)

    keep_sel = ones_where(rows_of(square) == kept)
    stays = dot_nt(field_high, keep_sel) + dot_nt(field_low, keep_sel)
    arrive = []
    start = counts[0:1, :]
    part_shape = (MOVE, elements)
    for slot in range(PEERS):
        number = rows_of(part_shape).astype(F32)
        count = counts[slot + 1 : slot + 2, :]
        hit = (lanes_of(part_shape).astype(F32) == start + number) & (number < count)
        arrive.append(jnp.where(hit, 1.0, 0.0))
        start = start + count
    arrive = jnp.concatenate(arrive, axis=0).astype(BF16)

    def arrived(ref):
        rows = jnp.concatenate([ref[slot] for slot in range(PEERS)], axis=0)
        high, low = split(rows.T)
        return dot(high, arrive) + dot(low, arrive)

    @pl.when(acoustic)
    def _():
        row_list[...] = jnp.full(row_list.shape, -1, jnp.int32)
        row_list[:, 0 : PEERS * FACE_CAP] = send_list[...]
        lane = rows_of((LANES, elements))
        entry = (PEERS - 1 - lane // FACE_CAP) * FACE_CAP + lane % FACE_CAP
        entry = jnp.where(lane < PEERS * FACE_CAP, entry + 6 * elements, -7)
        for face in range(6):
            slots = face_slot[face : face + 1, :]
            near[face] = ones_where(rows_of(square) + (face ^ 1) * elements == slots)
            far[:, elements * face : elements * face + elements] = ones_where(entry == slots)
            shape = (elements, LANES)
            sends[elements * face : elements * face + elements, :] = ones_where(
                rows_of(shape) + face * elements == row_list[...]
            )

    wait_recv_all(move_in, move_recv, move_send)
    out[...] = stays + arrived(move_in)

    @pl.when(acoustic)
    def _():
        lane = lanes_of((TRACE, LANES))
        for segment in range(SEGMENTS):

            def faces(slot):
                return peer_copy(
                    sent.at[segment], received.at[segment], face_send.at[segment], face_recv.at[segment], slot
                )

            high, low = split(out[...])
            shown = dot(pick[...], high) + dot(pick[...], low)
            shown_high, shown_low = split(shown)
            pairs = [
                jnp.concatenate(
                    [shown_high[TRACE * f : TRACE * f + TRACE], shown_low[TRACE * f : TRACE * f + TRACE]], axis=0
                )
                for f in range(6)
            ]
            listed = dot(jnp.concatenate(pairs, axis=1), sends[...])
            sent[segment] = listed[:TRACE] + listed[TRACE:]
            start_all(faces)
            rate = dot(own_high[...], high) + dot(own_high[...], low) + dot(own_low[...], high)
            local = [dot(pairs[f ^ 1], near[f]) for f in range(6)]
            if segment == 0:
                rows = lanes_of(square)
                source = ones_where(rows_of(square) == source_map[...])
                force_sel = dot_nt(move_sel, source).astype(BF16)
                stay_sel = dot_nt(source, keep_sel).astype(BF16)
                for chunk in range(3):
                    lamb_copy(chunk, 1).wait_recv()
                lamb_high, lamb_low = split(lamb[...])
                leaving = dot_nt(force_sel, lamb_high) + dot_nt(force_sel, lamb_low)
                for slot in range(PEERS):
                    force_out[slot] = leaving[MOVE * slot : MOVE * slot + MOVE, :]

                def forces(slot):
                    return peer_copy(force_out.at[slot], force_in, force_send, force_recv, slot)

                start_all(forces)
                stays_force = dot(lamb_high, stay_sel) + dot(lamb_low, stay_sel)
                wait_recv_all(force_in, force_recv, force_send)
                force[...] = stays_force + arrived(force_in)
            wait_recv_all(received.at[segment], face_recv.at[segment], face_send.at[segment])
            merged = jnp.zeros((TRACE, LANES), F32)
            for slot in range(PEERS):
                first = (PEERS - 1 - slot) * FACE_CAP
                here = (lane >= first) & (lane < first + FACE_CAP) & inside[slot]
                merged = jnp.where(here, received[segment, slot], merged)
            merged_high, merged_low = split(merged)
            remote = dot(jnp.concatenate([merged_high, merged_low], axis=0), far[...])
            outside = [local[f] + remote[:, elements * f : elements * f + elements] for f in range(6)]
            outside_high = jnp.concatenate([piece[:TRACE] for piece in outside], axis=0).astype(BF16)
            outside_low = jnp.concatenate([piece[TRACE:] for piece in outside], axis=0).astype(BF16)
            rate = rate + dot(lift[...], outside_high) + dot(lift[...], outside_low)
            rate = jnp.concatenate([rate[:64], rate[64:] + force[...]], axis=0)
            now = TIME_STEP * rate
            if segment > 0:
                now = SEGMENT_CARRY[segment] * carry[...] + now
            carry[...] = now
            out[...] = out[...] + SEGMENT_WEIGHTS[segment] * now

        for segment in range(SEGMENTS):
            wait_send_all(
                lambda slot: peer_copy(
                    sent.at[segment], received.at[segment], face_send.at[segment], face_recv.at[segment], slot
                )
            )
        wait_send_all(lambda slot: peer_copy(force_out.at[slot], force_in, force_send, force_recv, slot))

    wait_send_all(moves)

    @pl.when(flow)
    def _():
        for chunk in range(3):
            for other in range(1, n_sec):
                lamb_copy(chunk, other).wait_send()


def local(n_sec, n_dom, fields, source_map, new_owner, send_list, face_slot):
    rows = fields.shape[0] * fields.shape[1]
    elements = fields.shape[2]
    dma = pltpu.SemaphoreType.DMA
    vmem = pltpu.VMEM
    consts = [jnp.asarray(m) for m in constants()]
    call = pl.pallas_call(
        functools.partial(kernel, n_sec, n_dom),
        out_shape=jax.ShapeDtypeStruct((rows, elements), F32),
        in_specs=[pl.BlockSpec(memory_space=pltpu.VMEM)] * 10,
        out_specs=pl.BlockSpec(memory_space=pltpu.VMEM),
        scratch_shapes=[
            vmem((rows, elements), F32),
            vmem((192, elements), F32),
            vmem((192, elements), F32),
            vmem((6, elements, elements), BF16),
            vmem((LANES, 6 * elements), BF16),
            vmem((6 * elements, LANES), BF16),
            vmem((1, LANES), jnp.int32),
            vmem((PEERS, MOVE, rows), F32),
            vmem((PEERS, MOVE, rows), F32),
            vmem((PEERS, MOVE, 192), F32),
            vmem((PEERS, MOVE, 192), F32),
            vmem((SEGMENTS, TRACE, LANES), F32),
            vmem((SEGMENTS, PEERS, TRACE, LANES), F32),
            dma((3, n_sec - 1)),
            dma((3,)),
            dma((PEERS,)),
            dma((PEERS,)),
            dma((PEERS,)),
            dma((PEERS,)),
            dma((SEGMENTS, PEERS)),
            dma((SEGMENTS, PEERS)),
        ],
        compiler_params=pltpu.CompilerParams(
            collective_id=0, has_side_effects=True, vmem_limit_bytes=48 * 2**20
        ),
        name="step",
    )
    made = call(
        fields.reshape(rows, elements),
        source_map.reshape(1, -1),
        new_owner.reshape(1, -1),
        send_list.reshape(1, -1),
        face_slot,
        *consts,
    )
    return made.reshape(fields.shape)


def solution(mesh):
    both = ("sec", "dom")
    in_specs = (P(None, None, both), P(both), P(both), P(both), P(None, both))
    run = functools.partial(local, mesh.shape["sec"], mesh.shape["dom"])
    return jax.shard_map(
        run, mesh=mesh, in_specs=in_specs, out_specs=P(None, None, both), check_vma=False
    )
```

profile of v0, /device:TPU:7, one launch (start us, length us, event | category | flops | bytes accessed | tf_op | source)
XLA Modules:
  0.0 42.5 jit_solution(10004327790100000697)
XLA Ops:
  0.0 0.0 copy-start.9
  0.0 0.0 copy-start.7
  0.0 0.0 copy-start.8
  0.0 0.6 %copy-done.9 = s32[96]{0:T(128)S(1)} copy-done((s32[96]{0:T(128)S(1)}, s32[96]{0:T(128)}, u32[]{:S(2)}) %copy-start.9) | copy-done | bytes 408
  0.7 0.0 copy-done.7
  0.7 0.0 copy-done.8
  0.7 0.0 copy-start
  0.7 0.9 %copy-done = f32[4,64,256]{2,1,0:T(8,128)S(1)} copy-done((f32[4,64,256]{2,1,0:T(8,128)S(1)}, f32[4,64,256]{2,1,0:T(8,128)}, u32[]{:S(2)}) %copy-start) | copy-done | bytes 262168
  1.6 0.0 copy-start.1
  1.7 0.9 %copy-done.1 = bf16[256,288]{1,0:T(8,128)(2,1)S(1)} copy-done((bf16[256,288]{1,0:T(8,128)(2,1)S(1)}, bf16[256,288]{1,0:T(8,128)(2,1)}, u32[]{:S(2)}) %copy-start.1) | copy-done | bytes 147480
  2.6 0.0 copy-start.2
  2.6 0.9 %copy-done.2 = bf16[288,256]{1,0:T(8,128)(2,1)S(1)} copy-done((bf16[288,256]{1,0:T(8,128)(2,1)S(1)}, bf16[288,256]{1,0:T(8,128)(2,1)}, u32[]{:S(2)}) %copy-start.2) | copy-done | bytes 147480
  3.5 0.0 copy-start.3
  3.5 0.9 %copy-done.3 = bf16[256,256]{1,0:T(8,128)(2,1)S(1)} copy-done((bf16[256,256]{1,0:T(8,128)(2,1)S(1)}, bf16[256,256]{1,0:T(8,128)(2,1)}, u32[]{:S(2)}) %copy-start.3) | copy-done | bytes 131096
  4.4 0.0 copy-start.4
  4.4 0.9 %copy-done.4 = bf16[256,256]{1,0:T(8,128)(2,1)S(1)} copy-done((bf16[256,256]{1,0:T(8,128)(2,1)S(1)}, bf16[256,256]{1,0:T(8,128)(2,1)}, u32[]{:S(2)}) %copy-start.4) | copy-done | bytes 131096
  5.3 0.0 copy-start.5
  5.3 0.9 %copy-done.5 = bf16[192,192]{1,0:T(8,128)(2,1)S(1)} copy-done((bf16[192,192]{1,0:T(8,128)(2,1)S(1)}, bf16[192,192]{1,0:T(8,128)(2,1)}, u32[]{:S(2)}) %copy-start.5) | copy-done | bytes 73752
  6.2 0.0 copy-start.6
  6.2 0.7 %copy-done.6 = s32[6,256]{1,0:T(8,128)S(1)} copy-done((s32[6,256]{1,0:T(8,128)S(1)}, s32[6,256]{1,0:T(8,128)}, u32[]{:S(2)}) %copy-start.6) | copy-done | bytes 6168
  6.9 34.9 %step.1 = f32[256,256]{1,0:T(8,128)S(1)} custom-call(f32[256,256]{1,0:T(8,128)S(1)} %bitcast.6, s32[1,256]{1,0:T(1,128)S(1)} %bitcast.7, s32[1,64]{1,0:T(1,128)S(1)} %bitcast.8, s32[1,96]{1,0:T(1,128)S(1)} %bitcast.9, s32[6,256]{1,0:T(8,128)S(1)} %copy-done.6, bf16[256,256]{1,0:T(8,128)(2,1)S(1)} %copy-done.4, bf16[256,256]{1,0:T(8,128)(2,1)S(1)} %copy-done.3, ...), custom_call_target="tpu_custom_call" | custom-call | tf_op jit(solution)/shard_map/step/pallas_call | solution.py:437
  41.8 0.7 %copy.12 = f32[4,64,256]{2,1,0:T(8,128)} copy(f32[4,64,256]{2,1,0:T(8,128)S(1)} %bitcast.5) | data formatting | bytes 524288
Async XLA Ops:
  0.0 0.7 %copy-start.9 = (s32[96]{0:T(128)S(1)}, s32[96]{0:T(128)}, u32[]{:S(2)}) copy-start(s32[96]{0:T(128)} %param.13) | copy-start | bytes 1156
  0.0 0.7 %copy-start.7 = (s32[256]{0:T(256)S(1)}, s32[256]{0:T(256)}, u32[]{:S(2)}) copy-start(s32[256]{0:T(256)} %param.11) | copy-start | bytes 3076
  0.0 0.7 %copy-start.8 = (s32[64]{0:T(128)S(1)}, s32[64]{0:T(128)}, u32[]{:S(2)}) copy-start(s32[64]{0:T(128)} %param.12) | copy-start | bytes 772
  0.7 1.0 %copy-start = (f32[4,64,256]{2,1,0:T(8,128)S(1)}, f32[4,64,256]{2,1,0:T(8,128)}, u32[]{:S(2)}) copy-start(f32[4,64,256]{2,1,0:T(8,128)} %param.10) | copy-start | bytes 786436
  1.6 0.9 %copy-start.1 = (bf16[256,288]{1,0:T(8,128)(2,1)S(1)}, bf16[256,288]{1,0:T(8,128)(2,1)}, u32[]{:S(2)}) copy-start(bf16[256,288]{1,0:T(8,128)(2,1)} %constant.12.clone.lift) | copy-start | bytes 442372
  2.6 0.9 %copy-start.2 = (bf16[288,256]{1,0:T(8,128)(2,1)S(1)}, bf16[288,256]{1,0:T(8,128)(2,1)}, u32[]{:S(2)}) copy-start(bf16[288,256]{1,0:T(8,128)(2,1)} %constant.13.clone.pick) | copy-start | bytes 442372
  3.5 0.9 %copy-start.3 = (bf16[256,256]{1,0:T(8,128)(2,1)S(1)}, bf16[256,256]{1,0:T(8,128)(2,1)}, u32[]{:S(2)}) copy-start(bf16[256,256]{1,0:T(8,128)(2,1)} %constant.11.clone.own_low) | copy-start | bytes 393220
  4.4 0.9 %copy-start.4 = (bf16[256,256]{1,0:T(8,128)(2,1)S(1)}, bf16[256,256]{1,0:T(8,128)(2,1)}, u32[]{:S(2)}) copy-start(bf16[256,256]{1,0:T(8,128)(2,1)} %constant.10.clone.own_high) | copy-start | bytes 393220
  5.3 0.9 %copy-start.5 = (bf16[192,192]{1,0:T(8,128)(2,1)S(1)}, bf16[192,192]{1,0:T(8,128)(2,1)}, u32[]{:S(2)}) copy-start(bf16[192,192]{1,0:T(8,128)(2,1)} %constant.14.clone.curl) | copy-start | bytes 221188
  6.2 0.7 %copy-start.6 = (s32[6,256]{1,0:T(8,128)S(1)}, s32[6,256]{1,0:T(8,128)}, u32[]{:S(2)}) copy-start(s32[6,256]{1,0:T(8,128)} %face_slot.1) | copy-start | bytes 18436
where the time goes:
time: 42.8 us; the launch traced here: 42.5 us
  Pallas kernels  34.9 us (82%)
  local copies, waits for them, and re-layouts  7.58 us (18%)
    pallas_call x1, Pallas kernels, local(): call(fields.reshape(rows, elements), source_map.reshape(1, -1), new_owner...  34.9 us
    unnamed x21, local copies, waits for them, and re-layouts  7.58 us

commit v1 on v0

--- a/solution.py
+++ b/solution.py
@@ -16,6 +16,7 @@
 PEERS = 2 * SPREAD
 LANES = 128
 TRACE = 48
+SHOWN = 6 * TRACE
 OFFSETS = [value for value in range(-SPREAD, SPREAD + 1) if value != 0]
 
 CELL_DIFFERENCE = [
@@ -44,6 +45,10 @@
 F32 = jnp.float32
 BF16 = jnp.bfloat16
 MESH = pl.DeviceIdType.MESH
+INPUTS = 10
+CHUNKS = 4
+CHUNK_ROWS = 192 // CHUNKS
+FETCH_ORDER = (0, 2, 9, 1, 3, 4, 8, 5, 6, 7)
 
 
 def node_derivative():
@@ -105,14 +110,25 @@
         b, c = (a + 1) % 3, (a + 2) % 3
         curl[64 * a : 64 * a + 64, 64 * c : 64 * c + 64] += along(diff, b)
         curl[64 * a : 64 * a + 64, 64 * b : 64 * b + 64] -= along(diff, c)
-    own = own.astype(np.float32)
+    own = np.concatenate([pick @ own, own]).astype(np.float32)
+    lift = np.concatenate([pick @ lift, lift])
     own_high = own.astype(jnp.bfloat16)
     own_low = (own - own_high.astype(np.float32)).astype(jnp.bfloat16)
     return [m.astype(jnp.bfloat16) for m in (own_high, own_low, lift, pick, curl)]
 
 
-def slot_number(offset):
-    return offset + SPREAD if offset < 0 else offset + SPREAD - 1
+def lamb_routes(n_sec):
+    half = CHUNKS // 2
+    if n_sec < 4:
+        return [(0, other, chunk) for chunk in range(CHUNKS) for other in range(1, n_sec)]
+    last = n_sec - 1
+    routes = []
+    for chunk in range(CHUNKS):
+        for other in range(1, last):
+            routes.append((0, other, (chunk + half * (other - 1)) % CHUNKS))
+    for chunk in range(CHUNKS):
+        routes.append((1 if chunk < half else 2, last, chunk))
+    return routes
 
 
 def split(value):
@@ -142,13 +158,18 @@
 
 def kernel(
     n_sec, n_dom,
-    fields, source_map, new_owner, send_list, face_slot,
-    own_high, own_low, lift, pick, curl,
-    out,
-    carry, force, lamb, near, far, sends, row_list,
-    move_out, move_in, force_out, force_in, sent, received,
-    lamb_send, lamb_recv, move_send, move_recv, force_send, force_recv, face_send, face_recv,
+    *refs,
 ):
+    given, out, held = refs[:INPUTS], refs[INPUTS], refs[INPUTS + 1 : 2 * INPUTS + 1]
+    fields, source_map, new_owner, send_list, face_slot, own_high, own_low, lift, pick, curl = held
+    (
+        carry, force, shown, shown_carry, lamb, near, far, sends, row_list,
+        move_out, move_in, force_out, force_in, sent, received, in_sem,
+        lamb_send, lamb_recv, move_send, move_recv, force_send, force_recv, face_send, face_recv,
+    ) = refs[2 * INPUTS + 1 :]
+    fetch = [pltpu.make_async_copy(given[n], held[n], in_sem.at[n]) for n in range(INPUTS)]
+    for n in FETCH_ORDER:
+        fetch[n].start()
     sec, me = lax.axis_index("sec"), lax.axis_index("dom")
     elements = fields.shape[1]
     blocks = new_owner.shape[1]
@@ -157,7 +178,14 @@
     inside = [(me + o >= 0) & (me + o < n_dom) for o in OFFSETS]
 
     barrier = pltpu.get_barrier_semaphore()
-    greeted = jnp.where(flow, n_sec - 1, 1)
+    routes = lamb_routes(n_sec)
+    partners = {this: set() for this in range(n_sec)}
+    for source, target, chunk in routes:
+        partners[source].add(target)
+        partners[target].add(source)
+    greeted = 0
+    for this in range(n_sec):
+        greeted = greeted + jnp.where(sec == this, len(partners[this]), 0)
     for slot, o in enumerate(OFFSETS):
         greeted = greeted + jnp.where(inside[slot], 1, 0)
 
@@ -165,21 +193,19 @@
         def _():
             pl.semaphore_signal(barrier, inc=1, device_id=(sec, me + o), device_id_type=MESH)
 
-    @pl.when(flow)
-    def _():
-        for other in range(1, n_sec):
-            pl.semaphore_signal(barrier, inc=1, device_id=(other, me), device_id_type=MESH)
-
-    @pl.when(acoustic)
-    def _():
-        pl.semaphore_signal(barrier, inc=1, device_id=(0, me), device_id_type=MESH)
+    for this in range(n_sec):
+
+        @pl.when(sec == this)
+        def _():
+            for other in sorted(partners[this]):
+                pl.semaphore_signal(barrier, inc=1, device_id=(other, me), device_id_type=MESH)
 
     def lamb_copy(chunk, other):
-        part = lamb.at[pl.ds(64 * chunk, 64)]
+        part = lamb.at[pl.ds(CHUNK_ROWS * chunk, CHUNK_ROWS)]
         return pltpu.make_async_remote_copy(
             src_ref=part,
             dst_ref=part,
-            send_sem=lamb_send.at[chunk, other - 1],
+            send_sem=lamb_send.at[chunk, other],
             recv_sem=lamb_recv.at[chunk],
             device_id=(other, me),
             device_id_type=MESH,
@@ -223,6 +249,9 @@
             @pl.when(inside[slot])
             def _():
                 copies(slot).wait_send()
+
+    for n in range(INPUTS):
+        fetch[n].wait()
 
     @pl.when(flow)
     def _():
@@ -264,13 +293,13 @@
         return peer_copy(move_out.at[slot], move_in, move_send, move_recv, slot)
 
     pl.semaphore_wait(barrier, greeted)
-    start_all(moves)
-
     @pl.when(flow)
     def _():
-        for chunk in range(3):
-            for other in range(1, n_sec):
-                lamb_copy(chunk, other).start()
+        for source, target, chunk in routes:
+            if source == 0:
+                lamb_copy(chunk, target).start()
+
+    start_all(moves)
 
     for slot in range(PEERS):
 
@@ -313,6 +342,16 @@
                 rows_of(shape) + face * elements == row_list[...]
             )
 
+    relayed = {this: [(t, c) for source, t, c in routes if source == this] for this in range(1, n_sec)}
+    for this in range(1, n_sec):
+        if relayed[this]:
+
+            @pl.when(sec == this)
+            def _():
+                for target, chunk in relayed[this]:
+                    lamb_copy(chunk, target).wait_recv()
+                    lamb_copy(chunk, target).start()
+
     wait_recv_all(move_in, move_recv, move_send)
     out[...] = stays + arrived(move_in)
 
@@ -326,9 +365,10 @@
                     sent.at[segment], received.at[segment], face_send.at[segment], face_recv.at[segment], slot
                 )
 
-            high, low = split(out[...])
-            shown = dot(pick[...], high) + dot(pick[...], low)
-            shown_high, shown_low = split(shown)
+            if segment == 0:
+                high, low = split(out[...])
+                shown[...] = dot(pick[...], high) + dot(pick[...], low)
+            shown_high, shown_low = split(shown[...])
             pairs = [
                 jnp.concatenate(
                     [shown_high[TRACE * f : TRACE * f + TRACE], shown_low[TRACE * f : TRACE * f + TRACE]], axis=0
@@ -338,15 +378,27 @@
             listed = dot(jnp.concatenate(pairs, axis=1), sends[...])
             sent[segment] = listed[:TRACE] + listed[TRACE:]
             start_all(faces)
+            if segment > 0:
+                advance(segment - 1)
+                high, low = split(out[...])
+            beside = [dot(pairs[f ^ 1], near[f]) for f in range(6)]
+            beside_high = jnp.concatenate([piece[:TRACE] for piece in beside], axis=0).astype(BF16)
+            beside_low = jnp.concatenate([piece[TRACE:] for piece in beside], axis=0).astype(BF16)
             rate = dot(own_high[...], high) + dot(own_high[...], low) + dot(own_low[...], high)
-            local = [dot(pairs[f ^ 1], near[f]) for f in range(6)]
+            rate = rate + dot(lift[...], beside_high) + dot(lift[...], beside_low)
             if segment == 0:
-                rows = lanes_of(square)
                 source = ones_where(rows_of(square) == source_map[...])
                 force_sel = dot_nt(move_sel, source).astype(BF16)
                 stay_sel = dot_nt(source, keep_sel).astype(BF16)
-                for chunk in range(3):
-                    lamb_copy(chunk, 1).wait_recv()
+                for this in range(1, n_sec):
+
+                    @pl.when(sec == this)
+                    def _():
+                        early = [chunk for _, chunk in relayed[this]]
+                        for chunk in range(CHUNKS):
+                            if chunk not in early:
+                                lamb_copy(chunk, 0).wait_recv()
+
                 lamb_high, lamb_low = split(lamb[...])
                 leaving = dot_nt(force_sel, lamb_high) + dot_nt(force_sel, lamb_low)
                 for slot in range(PEERS):
@@ -358,7 +410,10 @@
                 start_all(forces)
                 stays_force = dot(lamb_high, stay_sel) + dot(lamb_low, stay_sel)
                 wait_recv_all(force_in, force_recv, force_send)
-                force[...] = stays_force + arrived(force_in)
+                forced = stays_force + arrived(force_in)
+                forced_high, forced_low = split(forced)
+                force[SHOWN:, :] = forced
+                force[:SHOWN, :] = dot(pick[:, 64:], forced_high) + dot(pick[:, 64:], forced_low)
             wait_recv_all(received.at[segment], face_recv.at[segment], face_send.at[segment])
             merged = jnp.zeros((TRACE, LANES), F32)
             for slot in range(PEERS):
@@ -367,16 +422,28 @@
                 merged = jnp.where(here, received[segment, slot], merged)
             merged_high, merged_low = split(merged)
             remote = dot(jnp.concatenate([merged_high, merged_low], axis=0), far[...])
-            outside = [local[f] + remote[:, elements * f : elements * f + elements] for f in range(6)]
-            outside_high = jnp.concatenate([piece[:TRACE] for piece in outside], axis=0).astype(BF16)
-            outside_low = jnp.concatenate([piece[TRACE:] for piece in outside], axis=0).astype(BF16)
-            rate = rate + dot(lift[...], outside_high) + dot(lift[...], outside_low)
-            rate = jnp.concatenate([rate[:64], rate[64:] + force[...]], axis=0)
-            now = TIME_STEP * rate
-            if segment > 0:
-                now = SEGMENT_CARRY[segment] * carry[...] + now
-            carry[...] = now
-            out[...] = out[...] + SEGMENT_WEIGHTS[segment] * now
+            remote = [remote[:, elements * f : elements * f + elements] for f in range(6)]
+            remote_high = jnp.concatenate([piece[:TRACE] for piece in remote], axis=0).astype(BF16)
+            remote_low = jnp.concatenate([piece[TRACE:] for piece in remote], axis=0).astype(BF16)
+            if segment < SEGMENTS - 1:
+                seen = rate[:SHOWN] + force[:SHOWN, :]
+                seen = seen + dot(lift[:SHOWN, :], remote_high) + dot(lift[:SHOWN, :], remote_low)
+                now = TIME_STEP * seen
+                if segment > 0:
+                    now = SEGMENT_CARRY[segment] * shown_carry[...] + now
+                shown_carry[...] = now
+                shown[...] = shown[...] + SEGMENT_WEIGHTS[segment] * now
+
+            def advance(number, rate=rate, remote_high=remote_high, remote_low=remote_low):
+                gain = rate[SHOWN:] + dot(lift[SHOWN:, :], remote_high) + dot(lift[SHOWN:, :], remote_low)
+                gain = jnp.concatenate([gain[:64], gain[64:] + force[SHOWN:, :]], axis=0)
+                step = TIME_STEP * gain
+                if number > 0:
+                    step = SEGMENT_CARRY[number] * carry[...] + step
+                carry[...] = step
+                out[...] = out[...] + SEGMENT_WEIGHTS[number] * step
+
+        advance(SEGMENTS - 1)
 
         for segment in range(SEGMENTS):
             wait_send_all(
@@ -388,11 +455,13 @@
 
     wait_send_all(moves)
 
-    @pl.when(flow)
-    def _():
-        for chunk in range(3):
-            for other in range(1, n_sec):
-                lamb_copy(chunk, other).wait_send()
+    for this in range(n_sec):
+
+        @pl.when(sec == this)
+        def _():
+            for source, target, chunk in routes:
+                if source == this:
+                    lamb_copy(chunk, target).wait_send()
 
 
 def local(n_sec, n_dom, fields, source_map, new_owner, send_list, face_slot):
@@ -401,14 +470,25 @@
     dma = pltpu.SemaphoreType.DMA
     vmem = pltpu.VMEM
     consts = [jnp.asarray(m) for m in constants()]
+    operands = [
+        fields.reshape(rows, elements),
+        source_map.reshape(1, -1),
+        new_owner.reshape(1, -1),
+        send_list.reshape(1, -1),
+        face_slot,
+        *consts,
+    ]
     call = pl.pallas_call(
         functools.partial(kernel, n_sec, n_dom),
         out_shape=jax.ShapeDtypeStruct((rows, elements), F32),
-        in_specs=[pl.BlockSpec(memory_space=pltpu.VMEM)] * 10,
+        in_specs=[pl.BlockSpec(memory_space=pltpu.HBM)] * INPUTS,
         out_specs=pl.BlockSpec(memory_space=pltpu.VMEM),
         scratch_shapes=[
+            *[vmem(value.shape, value.dtype) for value in operands],
             vmem((rows, elements), F32),
-            vmem((192, elements), F32),
+            vmem((SHOWN + 192, elements), F32),
+            vmem((SHOWN, elements), F32),
+            vmem((SHOWN, elements), F32),
             vmem((192, elements), F32),
             vmem((6, elements, elements), BF16),
             vmem((LANES, 6 * elements), BF16),
@@ -420,8 +500,9 @@
             vmem((PEERS, MOVE, 192), F32),
             vmem((SEGMENTS, TRACE, LANES), F32),
             vmem((SEGMENTS, PEERS, TRACE, LANES), F32),
-            dma((3, n_sec - 1)),
-            dma((3,)),
+            dma((INPUTS,)),
+            dma((CHUNKS, n_sec)),
+            dma((CHUNKS,)),
             dma((PEERS,)),
             dma((PEERS,)),
             dma((PEERS,)),
@@ -430,18 +511,11 @@
             dma((SEGMENTS, PEERS)),
         ],
         compiler_params=pltpu.CompilerParams(
-            collective_id=0, has_side_effects=True, vmem_limit_bytes=48 * 2**20
+            collective_id=0, has_side_effects=True, vmem_limit_bytes=63 * 2**20
         ),
         name="step",
     )
-    made = call(
-        fields.reshape(rows, elements),
-        source_map.reshape(1, -1),
-        new_owner.reshape(1, -1),
-        send_list.reshape(1, -1),
-        face_slot,
-        *consts,
-    )
+    made = call(*operands)
     return made.reshape(fields.shape)
 
 

time: 42.8 us -> 33.2 us (0.78)
  local copies, waits for them, and re-layouts: 7.58 us -> 1.67 us
  Pallas kernels: 34.9 us -> 31.3 us
    unnamed x21 -> x1, local copies, waits for them, and re-layouts: 7.58 us -> 1.67 us
    pallas_call x1, Pallas kernels: 34.9 us -> 31.3 us  [local(): made = call(*operands)]
where the time goes in v1:
time: 33.2 us; the launch traced here: 33 us
  Pallas kernels  31.3 us (94%)
  local copies, waits for them, and re-layouts  1.67 us (5%)
    pallas_call x1, Pallas kernels, local(): made = call(*operands)  31.3 us
    unnamed x1, local copies, waits for them, and re-layouts  1.67 us

profile of v1, /device:TPU:7, one launch (start us, length us, event | category | flops | bytes accessed | tf_op | source)
XLA Modules:
  0.0 33.0 jit_solution(1797205186077277777)
XLA Ops:
  0.0 31.3 %step.1 = f32[256,256]{1,0:T(8,128)} custom-call(f32[256,256]{1,0:T(8,128)} %bitcast.6, s32[1,256]{1,0:T(1,128)} %bitcast.7, s32[1,64]{1,0:T(1,128)} %bitcast.8, s32[1,96]{1,0:T(1,128)} %bitcast.9, s32[6,256]{1,0:T(8,128)} %refs_4_.1, bf16[544,256]{1,0:T(8,128)(2,1)} %constant.10.clone.refs_5_, bf16[544,256]{1,0:T(8,128)(2,1)} %constant.11.clone.refs_6_, ...), custom_call_target="tpu_custom_call" | custom-call | tf_op jit(solution)/shard_map/step/pallas_call | solution.py:518
  31.3 1.7 %copy.12 = f32[4,64,256]{2,1,0:T(8,128)} copy(f32[4,64,256]{2,1,0:T(8,128)} %bitcast.5) | data formatting | bytes 524288

commit v2 on v1

--- a/solution.py
+++ b/solution.py
@@ -48,7 +48,7 @@
 INPUTS = 10
 CHUNKS = 4
 CHUNK_ROWS = 192 // CHUNKS
-FETCH_ORDER = (0, 2, 9, 1, 3, 4, 8, 5, 6, 7)
+FETCH_ORDER = (0, 9, 2, 3, 4, 1, 8, 5, 6, 7)
 
 
 def node_derivative():
@@ -112,6 +112,7 @@
         curl[64 * a : 64 * a + 64, 64 * b : 64 * b + 64] -= along(diff, c)
     own = np.concatenate([pick @ own, own]).astype(np.float32)
     lift = np.concatenate([pick @ lift, lift])
+    lift = np.repeat(lift.reshape(-1, 6, 1, TRACE), 2, axis=2).reshape(-1, 2 * 6 * TRACE)
     own_high = own.astype(jnp.bfloat16)
     own_low = (own - own_high.astype(np.float32)).astype(jnp.bfloat16)
     return [m.astype(jnp.bfloat16) for m in (own_high, own_low, lift, pick, curl)]
@@ -250,8 +251,8 @@
             def _():
                 copies(slot).wait_send()
 
-    for n in range(INPUTS):
-        fetch[n].wait()
+    fetch[0].wait()
+    fetch[9].wait()
 
     @pl.when(flow)
     def _():
@@ -264,6 +265,15 @@
             b, c = (a + 1) % 3, (a + 2) % 3
             lamb[64 * a : 64 * a + 64, :] = rho * (w[b] * u[c] - w[c] * u[b])
 
+    pl.semaphore_wait(barrier, greeted)
+
+    @pl.when(flow)
+    def _():
+        for source, target, chunk in routes:
+            if source == 0:
+                lamb_copy(chunk, target).start()
+
+    fetch[2].wait()
     spread_shape = (blocks, elements)
     spread = ones_where(lanes_of(spread_shape) // BLOCK_SIZE == rows_of(spread_shape))
     owner = jnp.broadcast_to((new_owner[...] - me).astype(F32), (8, blocks)).astype(BF16)
@@ -292,14 +302,9 @@
     def moves(slot):
         return peer_copy(move_out.at[slot], move_in, move_send, move_recv, slot)
 
-    pl.semaphore_wait(barrier, greeted)
-    @pl.when(flow)
-    def _():
-        for source, target, chunk in routes:
-            if source == 0:
-                lamb_copy(chunk, target).start()
-
     start_all(moves)
+    for n in (1, 3, 4, 8, 5, 6, 7):
+        fetch[n].wait()
 
     for slot in range(PEERS):
 
@@ -382,10 +387,9 @@
                 advance(segment - 1)
                 high, low = split(out[...])
             beside = [dot(pairs[f ^ 1], near[f]) for f in range(6)]
-            beside_high = jnp.concatenate([piece[:TRACE] for piece in beside], axis=0).astype(BF16)
-            beside_low = jnp.concatenate([piece[TRACE:] for piece in beside], axis=0).astype(BF16)
+            beside_pair = jnp.concatenate(beside, axis=0).astype(BF16)
             rate = dot(own_high[...], high) + dot(own_high[...], low) + dot(own_low[...], high)
-            rate = rate + dot(lift[...], beside_high) + dot(lift[...], beside_low)
+            rate = rate + dot(lift[...], beside_pair)
             if segment == 0:
                 source = ones_where(rows_of(square) == source_map[...])
                 force_sel = dot_nt(move_sel, source).astype(BF16)
@@ -423,19 +427,18 @@
             merged_high, merged_low = split(merged)
             remote = dot(jnp.concatenate([merged_high, merged_low], axis=0), far[...])
             remote = [remote[:, elements * f : elements * f + elements] for f in range(6)]
-            remote_high = jnp.concatenate([piece[:TRACE] for piece in remote], axis=0).astype(BF16)
-            remote_low = jnp.concatenate([piece[TRACE:] for piece in remote], axis=0).astype(BF16)
+            remote_pair = jnp.concatenate(remote, axis=0).astype(BF16)
             if segment < SEGMENTS - 1:
                 seen = rate[:SHOWN] + force[:SHOWN, :]
-                seen = seen + dot(lift[:SHOWN, :], remote_high) + dot(lift[:SHOWN, :], remote_low)
+                seen = seen + dot(lift[:SHOWN, :], remote_pair)
                 now = TIME_STEP * seen
                 if segment > 0:
                     now = SEGMENT_CARRY[segment] * shown_carry[...] + now
                 shown_carry[...] = now
                 shown[...] = shown[...] + SEGMENT_WEIGHTS[segment] * now
 
-            def advance(number, rate=rate, remote_high=remote_high, remote_low=remote_low):
-                gain = rate[SHOWN:] + dot(lift[SHOWN:, :], remote_high) + dot(lift[SHOWN:, :], remote_low)
+            def advance(number, rate=rate, remote_pair=remote_pair):
+                gain = rate[SHOWN:] + dot(lift[SHOWN:, :], remote_pair)
                 gain = jnp.concatenate([gain[:64], gain[64:] + force[SHOWN:, :]], axis=0)
                 step = TIME_STEP * gain
                 if number > 0:

time: 33.2 us -> 31.9 us (0.961)
  Pallas kernels: 31.3 us -> 30 us
    pallas_call x1, Pallas kernels: 31.3 us -> 30 us  [local(): made = call(*operands)]
where the time goes in v2:
time: 31.9 us; the launch traced here: 31.7 us
  Pallas kernels  30 us (94%)
  local copies, waits for them, and re-layouts  1.67 us (5%)
    pallas_call x1, Pallas kernels, local(): made = call(*operands)  30 us
    unnamed x1, local copies, waits for them, and re-layouts  1.67 us

profile of v2, /device:TPU:7, one launch (start us, length us, event | category | flops | bytes accessed | tf_op | source)
XLA Modules:
  0.0 31.7 jit_solution(18139791500681554080)
XLA Ops:
  0.0 30.0 %step.1 = f32[256,256]{1,0:T(8,128)} custom-call(f32[256,256]{1,0:T(8,128)} %bitcast.6, s32[1,256]{1,0:T(1,128)} %bitcast.7, s32[1,64]{1,0:T(1,128)} %bitcast.8, s32[1,96]{1,0:T(1,128)} %bitcast.9, s32[6,256]{1,0:T(8,128)} %refs_4_.1, bf16[544,256]{1,0:T(8,128)(2,1)} %constant.10.clone.refs_5_, bf16[544,256]{1,0:T(8,128)(2,1)} %constant.11.clone.refs_6_, ...), custom_call_target="tpu_custom_call" | custom-call | tf_op jit(solution)/shard_map/step/pallas_call | solution.py:521
  30.0 1.7 %copy.12 = f32[4,64,256]{2,1,0:T(8,128)} copy(f32[4,64,256]{2,1,0:T(8,128)} %bitcast.5) | data formatting | bytes 524288

commit v3 on v2

--- a/solution.py
+++ b/solution.py
@@ -45,10 +45,10 @@
 F32 = jnp.float32
 BF16 = jnp.bfloat16
 MESH = pl.DeviceIdType.MESH
-INPUTS = 10
+INPUTS = 7
 CHUNKS = 4
 CHUNK_ROWS = 192 // CHUNKS
-FETCH_ORDER = (0, 9, 2, 3, 4, 1, 8, 5, 6, 7)
+FETCH_ORDER = (0, 5, 2, 3, 4, 1, 6)
 
 
 def node_derivative():
@@ -115,7 +115,9 @@
     lift = np.repeat(lift.reshape(-1, 6, 1, TRACE), 2, axis=2).reshape(-1, 2 * 6 * TRACE)
     own_high = own.astype(jnp.bfloat16)
     own_low = (own - own_high.astype(np.float32)).astype(jnp.bfloat16)
-    return [m.astype(jnp.bfloat16) for m in (own_high, own_low, lift, pick, curl)]
+    curl = np.pad(curl, ((0, 0), (0, 256 - curl.shape[1])))
+    square = np.concatenate([m.astype(jnp.bfloat16) for m in (curl, pick, own_high, own_low)])
+    return [square, lift.astype(jnp.bfloat16)]
 
 
 def lamb_routes(n_sec):
@@ -162,7 +164,11 @@
     *refs,
 ):
     given, out, held = refs[:INPUTS], refs[INPUTS], refs[INPUTS + 1 : 2 * INPUTS + 1]
-    fields, source_map, new_owner, send_list, face_slot, own_high, own_low, lift, pick, curl = held
+    fields, source_map, new_owner, send_list, face_slot, square_parts, lift = held
+    ends = (0, 192, 192 + SHOWN, 448 + 2 * SHOWN, 704 + 3 * SHOWN)
+    curl, pick, own_high, own_low = [
+        square_parts.at[pl.ds(ends[n], ends[n + 1] - ends[n])] for n in range(4)
+    ]
     (
         carry, force, shown, shown_carry, lamb, near, far, sends, row_list,
         move_out, move_in, force_out, force_in, sent, received, in_sem,
@@ -252,12 +258,12 @@
                 copies(slot).wait_send()
 
     fetch[0].wait()
-    fetch[9].wait()
+    fetch[5].wait()
 
     @pl.when(flow)
     def _():
         high, low = split(fields[0:192, :])
-        spin = dot(curl[...], high) + dot(curl[...], low)
+        spin = dot(curl[:, :192], high) + dot(curl[:, :192], low)
         u = [fields[64 * a : 64 * a + 64, :] for a in range(3)]
         w = [spin[64 * a : 64 * a + 64, :] for a in range(3)]
         rho = fields[192:256, :]
@@ -303,7 +309,7 @@
         return peer_copy(move_out.at[slot], move_in, move_send, move_recv, slot)
 
     start_all(moves)
-    for n in (1, 3, 4, 8, 5, 6, 7):
+    for n in (1, 3, 4, 6):
         fetch[n].wait()
 
     for slot in range(PEERS):

time: 31.9 us -> 31.9 us (level)
  no operation moved by 1% of the time
where the time goes in v3:
time: 31.9 us; the launch traced here: 31.7 us
  Pallas kernels  30 us (94%)
  local copies, waits for them, and re-layouts  1.67 us (5%)
    pallas_call x1, Pallas kernels, local(): made = call(*operands)  30 us
    unnamed x1, local copies, waits for them, and re-layouts  1.67 us

profile of v3, /device:TPU:7, one launch (start us, length us, event | category | flops | bytes accessed | tf_op | source)
XLA Modules:
  0.0 31.7 jit_solution(15553174170994985915)
XLA Ops:
  0.0 30.0 %step.1 = f32[256,256]{1,0:T(8,128)} custom-call(f32[256,256]{1,0:T(8,128)} %bitcast.6, s32[1,256]{1,0:T(1,128)} %bitcast.7, s32[1,64]{1,0:T(1,128)} %bitcast.8, s32[1,96]{1,0:T(1,128)} %bitcast.9, s32[6,256]{1,0:T(8,128)} %refs_4_.1, bf16[1568,256]{1,0:T(8,128)(2,1)} %constant.4.clone.refs_5_, bf16[544,576]{1,0:T(8,128)(2,1)} %constant.5.clone.refs_6_), custom_call_target="tpu_custom_call" | custom-call | tf_op jit(solution)/shard_map/step/pallas_call | solution.py:527
  30.1 1.7 %copy.9 = f32[4,64,256]{2,1,0:T(8,128)} copy(f32[4,64,256]{2,1,0:T(8,128)} %bitcast.5) | data formatting | bytes 524288
